TPU v7x, 32 devices: a whole 2x2x4 slice. The times are simulated.
32 devices in a mesh: band: 2 (over y), bl: 4 (over z), dir: 2 (over x), pol: 2 (over core).
Axes of the slice: x: 2, y: 2, z: 4, core: 2. Of those that a mesh axis runs over, the one named last changes fastest.
Arguments:
- visibilities: float32 [8, 4, 2, 32, 2, 4096], P('band', 'bl', 'pol'), parts along dimension 0, may hold values from -6 to 6
- hour_angle: float32 [4, 2, 32], P(None, 'pol'), may hold values from -1.5 to 1.5
- antenna_layout_coords: float32 [2, 2048], replicated, may hold values from -4 to 4
- point_coords: float32 [2, 2, 512], replicated, may hold values from -1 to 1
- point_flux: float32 [2, 512], replicated, may hold values from 0.01 to 0.1
- counts: int32 [2], replicated, may hold values from 128 to 512, as said below
- peel_order: int32 [2], replicated, may hold values from 0 to 1, each once
- earlier_gain_amplitude: float32 [4, 2048], P('band'), parts along dimension 0, may hold values from 0.5 to 1.5
- earlier_gain_phase: float32 [4, 2048], P('band'), parts along dimension 0, may hold values from -3.140625 to 3.140625
- tile_blocks: int32 [4, 2], P('bl'), may hold values from 0 to 31, as said below
Outputs:
- residual: float32 [8, 4, 2, 32, 2, 4096], P('band', 'bl', 'pol', 'dir'), parts along dimension 0
There are 2 independent parts, one for each index of `band`. A program takes and returns all parts, laid end to end along the dimension named above; an argument that names none is the same for every part. Nothing has to cross between parts.
Inputs may be any that keep to these rules, and one draw needn't show every extreme that they name: `tile_blocks`: each tile pairs two different antenna blocks. `counts`: one direction uses all 512 components.
All inputs are finite; a program needn't handle non-finite values.
Results may differ from a plain program's by a relative error of at most 0.002.
Values sent between devices are 32-bit elements; how exact they have to be, the bound alone decides.
A program may use at most 128 MiB of HBM per device.

v0:
```python
import jax
import jax.numpy as jnp
from jax import lax
from jax.sharding import PartitionSpec as P

NAB = 32
COMP = 512
ITERS = 3


LAMBDA = 1.0
TWO_PI = 6.283185307179586


def select_blocks(values, onehot):
    blocks = onehot.shape[1]
    grouped = values.reshape(values.shape[:-1] + (blocks, values.shape[-1] // blocks))
    return jnp.einsum("kn,...np->...kp", onehot, grouped, precision=lax.Precision.HIGHEST)


def phasors(positions, hour_values, coords):
    hour_cosine = jnp.cos(hour_values)[:, None, :, None]
    hour_sine = jnp.sin(hour_values)[:, None, :, None]
    east_pos = positions[0][None, :, None, :]
    north_pos = positions[1][None, :, None, :]
    coord_u = east_pos * hour_cosine - north_pos * hour_sine
    coord_v = east_pos * hour_sine + north_pos * hour_cosine
    phase_angle = TWO_PI * (coord_u[..., None] * coords[0] + coord_v[..., None] * coords[1])
    return (jnp.cos(phase_angle), jnp.sin(phase_angle))


def model_padded(left_pos, right_pos, hour_values, coords, weight):
    cos_left, sin_left = phasors(left_pos, hour_values, coords)
    cos_right, sin_right = phasors(right_pos, hour_values, coords)
    left_real_component = cos_left.astype(jnp.bfloat16)
    left_imag = sin_left.astype(jnp.bfloat16)
    stacked_right = jnp.concatenate(
        [(cos_right * weight).astype(jnp.bfloat16), (sin_right * weight).astype(jnp.bfloat16)],
        axis=-1,
    )
    real_left = jnp.concatenate([left_real_component, left_imag], axis=-1)
    left_imag_component = jnp.concatenate([left_imag, -left_real_component], axis=-1)
    einsum_form = "bktpc,bktqc->bktpq"
    model_real = jnp.einsum(
        einsum_form, real_left, stacked_right, preferred_element_type=jnp.float32
    )
    model_imag = jnp.einsum(
        einsum_form, left_imag_component, stacked_right, preferred_element_type=jnp.float32
    )
    full_shape = model_real.shape
    flat_shape = full_shape[:3] + (full_shape[3] * full_shape[4],)
    return (model_real.reshape(flat_shape), model_imag.reshape(flat_shape))


def outer_gains(left_real_component, left_imag, right_real, right_imag):
    outer_real = (
        left_real_component[..., :, None] * right_real[..., None, :]
        + left_imag[..., :, None] * right_imag[..., None, :]
    )
    outer_imag = (
        left_imag[..., :, None] * right_real[..., None, :]
        - left_real_component[..., :, None] * right_imag[..., None, :]
    )
    merged_shape = outer_real.shape[:-2] + (outer_real.shape[-2] * outer_real.shape[-1],)
    return (outer_real.reshape(merged_shape), outer_imag.reshape(merged_shape))


def peel_update(
    current, model_real, model_imag, prior_real, prior_imag, left_hot, right_hot, total_fn
):
    highest = lax.Precision.HIGHEST
    prior_outer = outer_gains(
        select_blocks(prior_real, left_hot),
        select_blocks(prior_imag, left_hot),
        select_blocks(prior_real, right_hot),
        select_blocks(prior_imag, right_hot),
    )
    outer_real = prior_outer[0][None, :, None, :]
    outer_imag = prior_outer[1][None, :, None, :]
    work_real = current[:, :, :, 0] + (outer_real * model_real - outer_imag * model_imag)
    work_imag = current[:, :, :, 1] + (outer_real * model_imag + outer_imag * model_real)
    batch_size = model_real.shape[0]
    tile_count = model_real.shape[1]
    tile_block_width = prior_real.shape[0] // left_hot.shape[1]
    square = (batch_size, tile_count, tile_block_width, tile_block_width)
    cross_real = jnp.sum(work_real * model_real + work_imag * model_imag, axis=2).reshape(square)
    cross_imag = jnp.sum(work_imag * model_real - work_real * model_imag, axis=2).reshape(square)
    model_power = jnp.sum(model_real * model_real + model_imag * model_imag, axis=2).reshape(square)
    gain_real = jnp.ones((batch_size, prior_real.shape[0]), jnp.float32)
    gain_imag = jnp.zeros((batch_size, prior_real.shape[0]), jnp.float32)
    row_form = "bkpq,bkq->bkp"
    column_form = "bkpq,bkp->bkq"
    for iteration in range(ITERS):
        left_real_component = select_blocks(gain_real, left_hot)
        left_imag = select_blocks(gain_imag, left_hot)
        right_real = select_blocks(gain_real, right_hot)
        right_imag = select_blocks(gain_imag, right_hot)
        left_terms = jnp.stack(
            [
                jnp.einsum(row_form, cross_real, right_real, precision=highest)
                - jnp.einsum(row_form, cross_imag, right_imag, precision=highest),
                jnp.einsum(row_form, cross_real, right_imag, precision=highest)
                + jnp.einsum(row_form, cross_imag, right_real, precision=highest),
                jnp.einsum(
                    row_form,
                    model_power,
                    right_real * right_real + right_imag * right_imag,
                    precision=highest,
                ),
            ],
            axis=1,
        )
        right_terms = jnp.stack(
            [
                jnp.einsum(column_form, cross_real, left_real_component, precision=highest)
                + jnp.einsum(column_form, cross_imag, left_imag, precision=highest),
                jnp.einsum(column_form, cross_real, left_imag, precision=highest)
                - jnp.einsum(column_form, cross_imag, left_real_component, precision=highest),
                jnp.einsum(
                    column_form,
                    model_power,
                    left_real_component * left_real_component + left_imag * left_imag,
                    precision=highest,
                ),
            ],
            axis=1,
        )
        normals = jnp.einsum("kn,bxkp->bxnp", left_hot, left_terms, precision=highest) + jnp.einsum(
            "kn,bxkp->bxnp", right_hot, right_terms, precision=highest
        )
        normals = total_fn(normals.reshape(batch_size, 3, prior_real.shape[0]))
        new_real = (normals[:, 0] + LAMBDA * gain_real) / (normals[:, 2] + LAMBDA)
        new_imag = (normals[:, 1] + LAMBDA * gain_imag) / (normals[:, 2] + LAMBDA)
        gain_real = 0.5 * (gain_real + new_real)
        gain_imag = 0.5 * (gain_imag + new_imag)
    final_outer = outer_gains(
        select_blocks(gain_real, left_hot),
        select_blocks(gain_imag, left_hot),
        select_blocks(gain_real, right_hot),
        select_blocks(gain_imag, right_hot),
    )
    fitted_real = final_outer[0][:, :, None, :]
    fitted_imag = final_outer[1][:, :, None, :]
    out_real = work_real - (fitted_real * model_real - fitted_imag * model_imag)
    out_imag = work_imag - (fitted_real * model_imag + fitted_imag * model_real)
    return jnp.stack([out_real, out_imag], axis=3)


def on_device(
    visibilities,
    hour_angle,
    antenna_layout_coords,
    point_coords,
    point_flux,
    counts,
    peel_order,
    earlier_gain_amplitude,
    earlier_gain_phase,
    tile_blocks,
):
    block_ids = jnp.arange(NAB, dtype=jnp.int32)[None, :]
    left_hot = (tile_blocks[:, 0:1] == block_ids).astype(jnp.float32)
    right_hot = (tile_blocks[:, 1:2] == block_ids).astype(jnp.float32)
    left_pos = select_blocks(antenna_layout_coords, left_hot)
    right_pos = select_blocks(antenna_layout_coords, right_hot)
    point_index = jnp.arange(COMP, dtype=jnp.int32)
    section = lax.axis_index("dir")
    sections = lax.axis_size("dir")
    states = visibilities[:, :, 0]
    hours_all = hour_angle[:, 0]

    def model_for(direction, hour_values):
        coords = lax.dynamic_index_in_dim(point_coords, direction, 0, keepdims=False)
        live_count = lax.dynamic_index_in_dim(counts, direction, 0, keepdims=False)
        weight = lax.dynamic_index_in_dim(point_flux, direction, 0, keepdims=False) * (
            point_index < live_count
        ).astype(jnp.float32)
        predicted = model_padded(left_pos, right_pos, hour_values, coords, weight)
        return predicted

    def peel_direction(current, hour_values, direction, total_fn):
        model_real, model_imag = model_for(direction, hour_values)
        amplitude = lax.dynamic_index_in_dim(earlier_gain_amplitude, direction, 0, keepdims=False)
        prior_angle = lax.dynamic_index_in_dim(earlier_gain_phase, direction, 0, keepdims=False)
        return peel_update(
            current,
            model_real,
            model_imag,
            amplitude * jnp.cos(prior_angle),
            amplitude * jnp.sin(prior_angle),
            left_hot,
            right_hot,
            total_fn,
        )

    own_times = states.shape[2] // sections

    def total_all(normals):
        return lax.psum(normals, ("bl", "dir", "pol"))

    own_states = lax.dynamic_slice_in_dim(states, section * own_times, own_times, 2)
    own_hours = lax.dynamic_slice_in_dim(hours_all, section * own_times, own_times, 1)

    def visit_section(position, current):
        direction = lax.dynamic_index_in_dim(peel_order, position, 0, keepdims=False)
        return peel_direction(current, own_hours, direction, total_all)

    my_share = lax.fori_loop(0, sections, visit_section, own_states)
    return my_share[:, :, None]


def solution(mesh):
    placed = (
        P("band", "bl", "pol", None, None, None),
        P(None, "pol", None),
        P(),
        P(),
        P(),
        P(),
        P(),
        P("band", None),
        P("band", None),
        P("bl", None),
    )
    return jax.shard_map(
        on_device,
        mesh=mesh,
        in_specs=placed,
        out_specs=P("band", "bl", "pol", "dir", None, None),
        check_vma=False,
    )
```

profile of v0, /device:TPU:0, one launch (start us, length us, event | category | flops | bytes accessed | tf_op | source)
XLA Modules:
  0.0 861.5 jit_solution(8376275828581980971)
XLA Ops:
  6.6 1.8 constant_dynamic-slice_fusion.3
  8.4 1.2 copy.89
  11.8 839.8 %while.16 = (s32[]{:T(128)}, f32[4,1,16,2,4096]{4,2,0,3,1:T(8,128)S(1)}, s32[2]{0:T(128)S(1)}, f32[2,2048]{1,0:T(2,128)S(1)}, f32[2,2048]{1,0:T(2,128)S(1)}, /*i...) while((s32[]{:T(128)}, ...), condition=%wide.region_7.8_spmd.clone, body=%wide.region_0.7_spmd.clone.sunk | while | flops 1205188608 | bytes 111450328 | solution.py:208
  17.7 1.1 fusion.457
  21.6 1.2 fusion.455
  22.7 3.1 squeeze.106
  25.8 2.2 squeeze.107
  28.8 31.4 %fusion.456 = bf16[4,1,16,64,512]{4,3,2,0,1:T(8,128)(2,1)} fusion(f32[512]{0:T(512)S(1)} %bitcast.842, f32[4,16,64]{2,1,0:T(8,128)S(1)} %get-tuple-element.601, f32[512]{0:T(512)S(1)} %bitcast.840, f32[4,16,64]{2,1,0:T(8,128)S(1)} %get-tuple-element.602), kind=kLoop, calls=%fused_computation.192.clone.1 | loop fusion | flops 16777216 | bytes 4231168 | tf_op jit(solution)/shard_map/while/body/eval_jaxpr/neg | solution.py:42
  60.2 67.6 %multiply_convert_fusion.3 = (bf16[4,1,16,64,512]{4,3,2,0,1:T(8,128)(2,1)S(1)}, bf16[4,1,16,64,512]{4,3,2,0,1:T(8,128)(2,1)S(1)}, bf16[4,1,16,64,512]{4,3,2,0,1:T(8,128)(2,1)}, bf16[4,1,16,64,512]{4,3,2,0,1:T(8,128)(2,1)}) fusion(f32[512]{0:T(512)S(1)} %fusion.453, f32[4,16,64]{2,1,0:T(8,128)S(1)} %get-tuple-element.597, ...), kind=kLoop, calls=%fused_computation.13.clone.1 | loop fusion | flops 29360128 | bytes 16848896 | tf_op jit(solution)/shard_map/while/body/eval_jaxpr/convert_element_type | solution.py:38
  127.9 7.0 fusion.454
  135.0 9.3 %subtract_reduce_fusion.2 = (f32[4,64,64]{2,1,0:T(8,128)S(1)}, f32[4,64,64]{2,1,0:T(8,128)S(1)}, f32[4,64,64]{2,1,0:T(8,128)S(1)}, f32[4,16,64,64]{3,2,1,0:T(8,128)}) fusion(f32[4,16,64,64]{3,2,1,0:T(8,128)S(1)} %fusion.454, f32[4,16,64,64]{3,2,1,0:T(8,128)} %squeeze.106, f32[4,16,64,64]{3,2,1,0:T(8,128)} %squeeze.107, ...), kind=kOutput, calls=%fused_computation.20.clone.1 | convolution fusion | flops 575619072 | bytes 21200896 | tf_op jit(solution)/shard_map/while/body/eval_jaxpr/bktpc,bktqc->bktpq/dot_general | solution.py:47
  148.7 0.8 reshape.1543
  149.5 89.9 %all-reduce.4.cloned.1.call-done = f32[4,3,2048]{2,0,1:T(4,128)} async-done(((f32[4,3,2048]{2,0,1:T(4,128)}), f32[4,3,2048]{2,0,1:T(4,128)}) %all-reduce.4.cloned.1.call-update) | async-done | bytes 98320 | tf_op jit(solution)/shard_map/while/body/eval_jaxpr/psum | solution.py:199
  239.4 0.8 add_multiply_fusion.4
  242.8 0.7 fusion.479
  246.3 0.8 reshape.1544
  247.7 85.7 %all-reduce.6.cloned.1.call-done = f32[4,3,2048]{2,0,1:T(4,128)} async-done(((f32[4,3,2048]{2,0,1:T(4,128)}), f32[4,3,2048]{2,0,1:T(4,128)}) %all-reduce.6.cloned.1.call-update) | async-done | bytes 98320 | tf_op jit(solution)/shard_map/while/body/eval_jaxpr/psum | solution.py:199
  333.4 0.8 fusion.486
  336.8 0.7 fusion.494
  340.3 0.8 reshape.1545
  341.1 2.1 reshape.1542
  343.2 2.9 reshape.1541
  346.1 81.2 %all-reduce.8.cloned.1.call-done = f32[4,3,2048]{2,0,1:T(4,128)} async-done(((f32[4,3,2048]{2,0,1:T(4,128)}), f32[4,3,2048]{2,0,1:T(4,128)}) %all-reduce.8.cloned.1.call-update) | async-done | bytes 98320 | tf_op jit(solution)/shard_map/while/body/eval_jaxpr/psum | solution.py:199
  427.3 0.8 fusion.501
  431.6 1.8 subtract_subtract_fusion.2
  439.4 1.1 fusion.457
  443.3 1.2 fusion.455
  444.5 3.1 squeeze.106
  447.6 2.2 squeeze.107
  450.6 31.4 %fusion.456 = bf16[4,1,16,64,512]{4,3,2,0,1:T(8,128)(2,1)} fusion(f32[512]{0:T(512)S(1)} %bitcast.842, f32[4,16,64]{2,1,0:T(8,128)S(1)} %get-tuple-element.601, f32[512]{0:T(512)S(1)} %bitcast.840, f32[4,16,64]{2,1,0:T(8,128)S(1)} %get-tuple-element.602), kind=kLoop, calls=%fused_computation.192.clone.1 | loop fusion | flops 16777216 | bytes 4231168 | tf_op jit(solution)/shard_map/while/body/eval_jaxpr/neg | solution.py:42
  482.0 67.6 %multiply_convert_fusion.3 = (bf16[4,1,16,64,512]{4,3,2,0,1:T(8,128)(2,1)S(1)}, bf16[4,1,16,64,512]{4,3,2,0,1:T(8,128)(2,1)S(1)}, bf16[4,1,16,64,512]{4,3,2,0,1:T(8,128)(2,1)}, bf16[4,1,16,64,512]{4,3,2,0,1:T(8,128)(2,1)}) fusion(f32[512]{0:T(512)S(1)} %fusion.453, f32[4,16,64]{2,1,0:T(8,128)S(1)} %get-tuple-element.597, ...), kind=kLoop, calls=%fused_computation.13.clone.1 | loop fusion | flops 29360128 | bytes 16848896 | tf_op jit(solution)/shard_map/while/body/eval_jaxpr/convert_element_type | solution.py:38
  549.6 7.0 fusion.454
  556.7 9.3 %subtract_reduce_fusion.2 = (f32[4,64,64]{2,1,0:T(8,128)S(1)}, f32[4,64,64]{2,1,0:T(8,128)S(1)}, f32[4,64,64]{2,1,0:T(8,128)S(1)}, f32[4,16,64,64]{3,2,1,0:T(8,128)}) fusion(f32[4,16,64,64]{3,2,1,0:T(8,128)S(1)} %fusion.454, f32[4,16,64,64]{3,2,1,0:T(8,128)} %squeeze.106, f32[4,16,64,64]{3,2,1,0:T(8,128)} %squeeze.107, ...), kind=kOutput, calls=%fused_computation.20.clone.1 | convolution fusion | flops 575619072 | bytes 21200896 | tf_op jit(solution)/shard_map/while/body/eval_jaxpr/bktpc,bktqc->bktpq/dot_general | solution.py:47
  570.4 0.8 reshape.1543
  571.3 86.2 %all-reduce.4.cloned.1.call-done = f32[4,3,2048]{2,0,1:T(4,128)} async-done(((f32[4,3,2048]{2,0,1:T(4,128)}), f32[4,3,2048]{2,0,1:T(4,128)}) %all-reduce.4.cloned.1.call-update) | async-done | bytes 98320 | tf_op jit(solution)/shard_map/while/body/eval_jaxpr/psum | solution.py:199
  657.5 0.8 add_multiply_fusion.4
  660.9 0.7 fusion.479
  664.4 0.8 reshape.1544
  665.7 85.7 %all-reduce.6.cloned.1.call-done = f32[4,3,2048]{2,0,1:T(4,128)} async-done(((f32[4,3,2048]{2,0,1:T(4,128)}), f32[4,3,2048]{2,0,1:T(4,128)}) %all-reduce.6.cloned.1.call-update) | async-done | bytes 98320 | tf_op jit(solution)/shard_map/while/body/eval_jaxpr/psum | solution.py:199
  751.5 0.8 fusion.486
  754.8 0.7 fusion.494
  758.3 0.8 reshape.1545
  759.1 2.1 reshape.1542
  761.3 2.9 reshape.1541
  764.2 81.2 %all-reduce.8.cloned.1.call-done = f32[4,3,2048]{2,0,1:T(4,128)} async-done(((f32[4,3,2048]{2,0,1:T(4,128)}), f32[4,3,2048]{2,0,1:T(4,128)}) %all-reduce.8.cloned.1.call-update) | async-done | bytes 98320 | tf_op jit(solution)/shard_map/while/body/eval_jaxpr/psum | solution.py:199
  845.4 0.8 fusion.501
  849.7 1.8 subtract_subtract_fusion.2
  851.7 2.9 copy.88
  (273 shorter events, 55.4 us)
Async XLA Ops:
  6.5 3.1 copy-start.9
  6.5 3.2 copy-start.11
  6.5 4.4 copy-start.10
  6.5 5.3 copy-start.2
  6.5 5.3 copy-start.3
  6.5 5.3 copy-start.4
  6.6 5.3 copy-start.12
  6.6 5.3 copy-start.14
  11.9 16.8 %copy-start.5 = (f32[2,1,64]{2,1,0:T(1,128)}, f32[2,1,64]{2,1,0:T(1,128)S(1)}, u32[]{:S(2)}) copy-start(f32[2,1,64]{2,1,0:T(1,128)S(1)} %get-tuple-element.674) | copy-start | bytes 1540 | tf_op jit(solution)/shard_map/while
  11.9 16.8 %copy-start.7 = (f32[2,1,64]{2,1,0:T(1,128)}, f32[2,1,64]{2,1,0:T(1,128)S(1)}, u32[]{:S(2)}) copy-start(f32[2,1,64]{2,1,0:T(1,128)S(1)} %get-tuple-element.678) | copy-start | bytes 1540 | tf_op jit(solution)/shard_map/while
  11.9 227.5 %all-reduce.4.cloned.1.call-start = ((), (), s32[]{:S(2)}) async-start(), calls=%async_computation | async-start | bytes 196608 | tf_op jit(solution)/shard_map/while/body/eval_jaxpr/psum | solution.py:199
  127.9 7.0 copy-start
  134.9 9.4 %copy-start.1 = (f32[4,16,64,64]{3,2,1,0:T(8,128)}, f32[4,16,64,64]{3,2,1,0:T(8,128)S(1)}, u32[]{:S(2)}) copy-start(f32[4,16,64,64]{3,2,1,0:T(8,128)S(1)} %fusion.454) | copy-start | bytes 3145732 | tf_op jit(solution)/shard_map/while
  149.5 183.9 %all-reduce.6.cloned.1.call-start = ((), (), s32[]{:S(2)}) async-start(), calls=%async_computation.1 | async-start | bytes 196608 | tf_op jit(solution)/shard_map/while/body/eval_jaxpr/psum | solution.py:199
  247.1 180.2 %all-reduce.8.cloned.1.call-start = ((), (), s32[]{:S(2)}) async-start(), calls=%async_computation.2 | async-start | bytes 196608 | tf_op jit(solution)/shard_map/while/body/eval_jaxpr/psum | solution.py:199
  431.6 2.0 copy-start.6
  431.6 2.0 copy-start.8
  431.6 2.0 copy-start.13
  431.6 2.0 copy-start.15
  433.6 16.8 %copy-start.5 = (f32[2,1,64]{2,1,0:T(1,128)}, f32[2,1,64]{2,1,0:T(1,128)S(1)}, u32[]{:S(2)}) copy-start(f32[2,1,64]{2,1,0:T(1,128)S(1)} %get-tuple-element.674) | copy-start | bytes 1540 | tf_op jit(solution)/shard_map/while
  433.6 16.8 %copy-start.7 = (f32[2,1,64]{2,1,0:T(1,128)}, f32[2,1,64]{2,1,0:T(1,128)S(1)}, u32[]{:S(2)}) copy-start(f32[2,1,64]{2,1,0:T(1,128)S(1)} %get-tuple-element.678) | copy-start | bytes 1540 | tf_op jit(solution)/shard_map/while
  433.6 223.9 %all-reduce.4.cloned.1.call-start = ((), (), s32[]{:S(2)}) async-start(), calls=%async_computation | async-start | bytes 196608 | tf_op jit(solution)/shard_map/while/body/eval_jaxpr/psum | solution.py:199
  549.6 7.0 copy-start
  556.6 9.4 %copy-start.1 = (f32[4,16,64,64]{3,2,1,0:T(8,128)}, f32[4,16,64,64]{3,2,1,0:T(8,128)S(1)}, u32[]{:S(2)}) copy-start(f32[4,16,64,64]{3,2,1,0:T(8,128)S(1)} %fusion.454) | copy-start | bytes 3145732 | tf_op jit(solution)/shard_map/while
  571.2 180.2 %all-reduce.6.cloned.1.call-start = ((), (), s32[]{:S(2)}) async-start(), calls=%async_computation.1 | async-start | bytes 196608 | tf_op jit(solution)/shard_map/while/body/eval_jaxpr/psum | solution.py:199
  665.1 180.2 %all-reduce.8.cloned.1.call-start = ((), (), s32[]{:S(2)}) async-start(), calls=%async_computation.2 | async-start | bytes 196608 | tf_op jit(solution)/shard_map/while/body/eval_jaxpr/psum | solution.py:199
  849.7 2.0 copy-start.6
  849.7 2.0 copy-start.8
  849.7 2.0 copy-start.13
  849.7 2.0 copy-start.15
Sparse Core Ops, SparseCore 0:
  149.6 89.7 all-reduce.3
  247.2 86.1 all-reduce.5
  341.2 86.0 all-reduce.7
  571.4 86.0 all-reduce.3
  665.3 86.1 all-reduce.5
  759.3 86.0 all-reduce.7
where the time goes:
time: 863 us; the launch traced here: 861 us
  waiting for transfers between devices  510 us (59%)
  other arithmetic  213 us (25%)
  matrix products  79 us (9%)
  local copies, waits for them, and re-layouts  41.3 us (5%)
  between operations  13.5 us (2%)
    psum x6, waiting for transfers between devices, total_all(): return lax.psum(normals, ('bl', 'dir', 'pol'))  510 us
    convert_element_type x2, other arithmetic, model_padded(): (cos_right * weight).astype(jnp.bfloat16)  135 us
    neg x2, other arithmetic, model_padded(): -left_real_component  62.8 us
    dot_general x42, matrix products, select_blocks(): jnp.einsum('kn,...np->...kp', onehot, grouped, precision=lax.Precision.HI...  29.8 us
    dot_general x2, matrix products, model_padded(): jnp.einsum(einsum_form, left_imag_component, stacked_right, preferred_ele...  18.7 us
  transfers between devices with their start and end apart: 6, of which 6 were waited for; matrix products, arithmetic and copies ran while one was open for 1% of the time, Pallas kernels for 0%

commit v1 on v0

v1 whole, which is shorter than its diff:
```python
import functools

import jax
import jax.numpy as jnp
from jax import lax
from jax.experimental import pallas as pl
from jax.experimental.pallas import tpu as pltpu
from jax.sharding import PartitionSpec as P

ABLK = 64
ITERS = 3
LAMBDA = 1.0
HALF = ABLK // 2
LANES = 2 * ABLK
CHUNK = 128
MESH = pl.DeviceIdType.MESH
HIGHEST = lax.Precision.HIGHEST
SIN_C = (4.442867911308811, -7.307443741853454, 3.5947910749268956, -0.784381842458349)
COS_C = (1.4142040873683897, -6.977642700991201, 5.715246760161864, -1.7283748369726175)


def half_turns(turns):
    part = turns - jnp.round(turns)
    square = part * part
    sine = SIN_C[-1]
    for value in SIN_C[-2::-1]:
        sine = sine * square + value
    cosine = COS_C[-1]
    for value in COS_C[-2::-1]:
        cosine = cosine * square + value
    return part * sine, cosine


def swap_halves(values):
    return pltpu.roll(values, ABLK, 1)


def predict_sample(chunks, pos_ref, east_row, north_row, weight_row):
    left_cos, left_sin, right_cos, right_sin = [], [], [], []
    for chunk in range(chunks):
        lanes = slice(chunk * CHUNK, (chunk + 1) * CHUNK)
        east, north, weight = east_row[:, lanes], north_row[:, lanes], weight_row[:, lanes]
        sine, cosine = half_turns(pos_ref[0] * east + pos_ref[1] * north)
        left_cos.append((1.0 - sine * sine).astype(jnp.bfloat16))
        left_sin.append((sine * cosine).astype(jnp.bfloat16))
        sine, cosine = half_turns(pos_ref[2] * east + pos_ref[3] * north)
        weighted = sine * weight
        right_cos.append((weight - weighted * sine).astype(jnp.bfloat16))
        right_sin.append((weighted * cosine).astype(jnp.bfloat16))
    left = jnp.concatenate(
        [jnp.concatenate(left_cos, axis=1), jnp.concatenate(left_sin, axis=1)], axis=0
    )
    right = jnp.concatenate(
        [jnp.concatenate(right_cos, axis=1), jnp.concatenate(right_sin, axis=1)], axis=0
    )
    out = lax.dot_general(
        left, right, (((1,), (1,)), ((), ())), preferred_element_type=jnp.float32
    )
    cos_even, cos_odd = out[:HALF], out[HALF:ABLK]
    sin_even, sin_odd = out[ABLK : ABLK + HALF], out[ABLK + HALF :]
    first = lax.broadcasted_iota(jnp.int32, (HALF, LANES), 1) < ABLK
    real = jnp.where(first, cos_even, swap_halves(cos_odd)) + jnp.where(
        first, swap_halves(sin_even), sin_odd
    )
    imag = jnp.where(first, sin_even, swap_halves(sin_odd)) - jnp.where(
        first, swap_halves(cos_even), cos_odd
    )
    return real, imag


def model_kernel(
    sections,
    times,
    comps,
    unroll,
    scalars,
    pos_ref,
    east_ref,
    north_ref,
    weight_ref,
    prior_ref,
    vis_ref,
    model_ref,
    sums_ref,
):
    def one_section(section):
        weight_row = weight_ref[section]

        def run(chunks):
            def sample(time, carry):
                real, imag = predict_sample(
                    chunks,
                    pos_ref,
                    east_ref[0, section, pl.ds(time, 1), :],
                    north_ref[0, section, pl.ds(time, 1), :],
                    weight_row,
                )
                model_ref[0, section, time, 0] = real
                model_ref[0, section, time, 1] = imag
                return carry

            lax.fori_loop(0, times, sample, 0, unroll=unroll)

        for chunks in range(1, comps // CHUNK + 1):
            pl.when(scalars[1 + section] == chunks)(functools.partial(run, chunks))

    if sections <= 2:
        for section in range(sections):
            one_section(section)
    else:
        lax.fori_loop(0, sections, lambda s, c: (one_section(s), c)[1], 0)

    zero = jnp.zeros((HALF, LANES), jnp.float32)
    pair = 3 * sections
    for section in range(sections):

        def with_vis(time, carry):
            cross_real, cross_imag, power = carry
            real, imag = model_ref[0, section, time, 0], model_ref[0, section, time, 1]
            vis_real = vis_ref[0, time, pl.ds(0, HALF, 2), :]
            vis_imag = vis_ref[0, time, pl.ds(1, HALF, 2), :]
            return (
                cross_real + (vis_real * real + vis_imag * imag),
                cross_imag + (vis_imag * real - vis_real * imag),
                power + (real * real + imag * imag),
            )

        cross_real, cross_imag, power = lax.fori_loop(0, times, with_vis, (zero, zero, zero))
        cross_real += prior_ref[section, 0] * power
        cross_imag += prior_ref[section, 1] * power
        for other in range(section):

            def with_model(time, carry):
                pair_real, pair_imag = carry
                real, imag = model_ref[0, section, time, 0], model_ref[0, section, time, 1]
                other_real, other_imag = model_ref[0, other, time, 0], model_ref[0, other, time, 1]
                return (
                    pair_real + (other_real * real + other_imag * imag),
                    pair_imag + (other_imag * real - other_real * imag),
                )

            pair_real, pair_imag = lax.fori_loop(0, times, with_model, (zero, zero))
            prior_real, prior_imag = prior_ref[other, 0], prior_ref[other, 1]
            cross_real += prior_real * pair_real - prior_imag * pair_imag
            cross_imag += prior_real * pair_imag + prior_imag * pair_real
            sums_ref[0, pl.ds(pair * HALF, HALF), :] = pair_real
            sums_ref[0, pl.ds((pair + 1) * HALF, HALF), :] = pair_imag
            pair += 2
        sums_ref[0, pl.ds(3 * section * HALF, HALF), :] = cross_real
        sums_ref[0, pl.ds((3 * section + 1) * HALF, HALF), :] = cross_imag
        sums_ref[0, pl.ds((3 * section + 2) * HALF, HALF), :] = power


def each(count, body):
    if count <= 4:
        for index in range(count):
            body(index)
    else:
        lax.fori_loop(0, count, lambda index, carry: (body(index), carry)[1], 0)


def solve_kernel(
    sections,
    intervals,
    tiles,
    dirs,
    pols,
    sums_ref,
    ids_ref,
    out_ref,
    part_ref,
    tile_ref,
    gain_msg_ref,
    square_ref,
    gain_ref,
    normal_ref,
    final_ref,
    part_send,
    part_recv,
    tile_send,
    tile_recv,
    gain_send,
    gain_recv,
):
    group = dirs * pols
    rows = sums_ref.shape[1]
    here = lax.axis_index("bl")
    me = lax.axis_index("dir") * pols + lax.axis_index("pol")

    def group_peer(step):
        peer = lax.rem(me + step, group)
        return peer, {"dir": peer // pols, "pol": lax.rem(peer, pols)}

    barrier = pltpu.get_barrier_semaphore()
    for step in range(1, group):
        pl.semaphore_signal(barrier, inc=1, device_id=group_peer(step)[1], device_id_type=MESH)
    for step in range(1, tiles):
        pl.semaphore_signal(
            barrier, inc=1, device_id={"bl": lax.rem(here + step, tiles)}, device_id_type=MESH
        )
    pl.semaphore_wait(barrier, group - 1 + tiles - 1)

    copies = []
    for step in range(1, group):
        peer, where = group_peer(step)
        copies.append(
            pltpu.make_async_remote_copy(
                src_ref=sums_ref.at[lax.rem(peer, intervals)],
                dst_ref=part_ref.at[step - 1],
                send_sem=part_send.at[step - 1],
                recv_sem=part_recv.at[step - 1],
                device_id=where,
                device_id_type=MESH,
            )
        )
        copies[-1].start()
    total = sums_ref[lax.rem(me, intervals)]
    for step in range(1, group):
        copies[step - 1].wait_recv()
        total += part_ref[step - 1]
    tile_ref[here, pl.ds(0, rows), :] = total
    tile_ref[here, pl.ds(rows, 8), :] = ids_ref[...]
    for copy in copies:
        copy.wait_send()

    copies = []
    for step in range(1, tiles):
        copies.append(
            pltpu.make_async_remote_copy(
                src_ref=tile_ref.at[here],
                dst_ref=tile_ref.at[here],
                send_sem=tile_send.at[step - 1],
                recv_sem=tile_recv.at[step - 1],
                device_id={"bl": lax.rem(here + step, tiles)},
                device_id_type=MESH,
            )
        )
        copies[-1].start()
    for copy in copies:
        copy.wait()

    sides = 2 * tiles
    ids = jnp.concatenate(
        [tile_ref[k, pl.ds(rows, 1), :] for k in range(tiles)]
        + [tile_ref[k, pl.ds(rows + 1, 1), :] for k in range(tiles)],
        axis=0,
    )[:, :ABLK]

    def shared_sum(values):
        total = jnp.zeros((sides, ABLK), jnp.float32)
        for side in range(sides):
            total += jnp.where(ids == ids[side : side + 1], values[side : side + 1], 0.0)
        return total

    def unpack(tile, slot, index):
        packed = tile_ref[tile, pl.ds(index * HALF, HALF), :]
        square_ref[tile, slot, pl.ds(0, HALF, 2), :] = packed
        square_ref[tile, slot, pl.ds(1, HALF, 2), :] = swap_halves(packed)

    def side_rows(real, imag):
        return jnp.concatenate(
            [real, imag, real * real + imag * imag, jnp.zeros((5, ABLK), jnp.float32)], axis=0
        )

    pair = 3 * sections
    for section in range(sections):

        def load_tile(tile):
            for slot in range(3):
                unpack(tile, slot, 3 * section + slot)

        each(tiles, load_tile)
        for other in range(section):

            def take_off(tile, other=other, pair=pair):
                unpack(tile, 3, pair)
                unpack(tile, 4, pair + 1)
                left_real = final_ref[other, 0, pl.ds(tile, 1), :]
                left_imag = final_ref[other, 1, pl.ds(tile, 1), :]
                right_real = final_ref[other, 0, pl.ds(tiles + tile, 1), :]
                right_imag = final_ref[other, 1, pl.ds(tiles + tile, 1), :]
                tall = jnp.concatenate(
                    [left_real, left_imag, jnp.zeros((6, ABLK), jnp.float32)], axis=0
                )
                zeros = jnp.zeros((6, ABLK), jnp.float32)
                form = (((0,), (0,)), ((), ()))
                outer_real = lax.dot_general(
                    tall,
                    jnp.concatenate([right_real, right_imag, zeros], axis=0),
                    form,
                    precision=HIGHEST,
                    preferred_element_type=jnp.float32,
                )
                outer_imag = lax.dot_general(
                    tall,
                    jnp.concatenate([-right_imag, right_real, zeros], axis=0),
                    form,
                    precision=HIGHEST,
                    preferred_element_type=jnp.float32,
                )
                pair_real = square_ref[tile, 3, :, pl.ds(0, ABLK)]
                pair_imag = square_ref[tile, 4, :, pl.ds(0, ABLK)]
                square_ref[tile, 0, :, pl.ds(0, ABLK)] -= (
                    outer_real * pair_real - outer_imag * pair_imag
                )
                square_ref[tile, 1, :, pl.ds(0, ABLK)] -= (
                    outer_real * pair_imag + outer_imag * pair_real
                )

            each(tiles, take_off)
            pair += 2

        gain_ref[0] = jnp.ones((sides, ABLK), jnp.float32)
        gain_ref[1] = jnp.zeros((sides, ABLK), jnp.float32)
        for _ in range(ITERS):

            def tile_normals(tile):
                cross_real = square_ref[tile, 0, :, pl.ds(0, ABLK)]
                cross_imag = square_ref[tile, 1, :, pl.ds(0, ABLK)]
                power = square_ref[tile, 2, :, pl.ds(0, ABLK)]
                from_right = side_rows(
                    gain_ref[0, pl.ds(tiles + tile, 1), :], gain_ref[1, pl.ds(tiles + tile, 1), :]
                )
                from_left = side_rows(
                    gain_ref[0, pl.ds(tile, 1), :], gain_ref[1, pl.ds(tile, 1), :]
                )

                def along(values, matrix, dim):
                    return lax.dot_general(
                        values,
                        matrix,
                        (((1,), (dim,)), ((), ())),
                        precision=HIGHEST,
                        preferred_element_type=jnp.float32,
                    )

                by_real, by_imag = along(from_right, cross_real, 1), along(from_right, cross_imag, 1)
                normal_ref[0, pl.ds(tile, 1), :] = by_real[0:1] - by_imag[1:2]
                normal_ref[1, pl.ds(tile, 1), :] = by_real[1:2] + by_imag[0:1]
                normal_ref[2, pl.ds(tile, 1), :] = along(from_right, power, 1)[2:3]
                by_real, by_imag = along(from_left, cross_real, 0), along(from_left, cross_imag, 0)
                normal_ref[0, pl.ds(tiles + tile, 1), :] = by_real[0:1] + by_imag[1:2]
                normal_ref[1, pl.ds(tiles + tile, 1), :] = by_real[1:2] - by_imag[0:1]
                normal_ref[2, pl.ds(tiles + tile, 1), :] = along(from_left, power, 0)[2:3]

            each(tiles, tile_normals)
            gain_real, gain_imag = gain_ref[0], gain_ref[1]
            below = shared_sum(normal_ref[2]) + LAMBDA
            gain_ref[0] = 0.5 * (
                gain_real + (shared_sum(normal_ref[0]) + LAMBDA * gain_real) / below
            )
            gain_ref[1] = 0.5 * (
                gain_imag + (shared_sum(normal_ref[1]) + LAMBDA * gain_imag) / below
            )
        final_ref[section] = gain_ref[...]

    for section in range(sections):
        for row, (kind, side) in enumerate(((0, here), (1, here), (0, tiles + here), (1, tiles + here))):
            gain_msg_ref[me, section, pl.ds(row, 1), pl.ds(0, ABLK)] = final_ref[
                section, kind, pl.ds(side, 1), :
            ]
    copies = []
    for step in range(1, group):
        copies.append(
            pltpu.make_async_remote_copy(
                src_ref=gain_msg_ref.at[me],
                dst_ref=gain_msg_ref.at[me],
                send_sem=gain_send.at[step - 1],
                recv_sem=gain_recv.at[step - 1],
                device_id=group_peer(step)[1],
                device_id_type=MESH,
            )
        )
        copies[-1].start()
    for copy in copies:
        copy.wait()
    for interval in range(intervals):
        out_ref[interval] = gain_msg_ref[interval, :, pl.ds(0, 4), pl.ds(0, ABLK)]


def residual_kernel(sections, times, scalars, vis_ref, model_ref, factor_ref, out_ref):
    def sample(time, carry):
        real = vis_ref[0, time, pl.ds(0, HALF, 2), :]
        imag = vis_ref[0, time, pl.ds(1, HALF, 2), :]
        for section in range(sections):
            model_real = model_ref[0, section, time, 0]
            model_imag = model_ref[0, section, time, 1]
            factor_real, factor_imag = factor_ref[0, section, 0], factor_ref[0, section, 1]
            real += factor_real * model_real - factor_imag * model_imag
            imag += factor_real * model_imag + factor_imag * model_real
        out_ref[0, time, pl.ds(0, HALF, 2), :] = real
        out_ref[0, time, pl.ds(1, HALF, 2), :] = imag
        return carry

    lax.fori_loop(0, times, sample, 0)


def outer_gains(left_real, left_imag, right_real, right_imag):
    real = left_real[..., :, None] * right_real[..., None, :] + (
        left_imag[..., :, None] * right_imag[..., None, :]
    )
    imag = left_imag[..., :, None] * right_real[..., None, :] - (
        left_real[..., :, None] * right_imag[..., None, :]
    )
    both = jnp.stack([real, imag], axis=-3)
    return both.reshape(both.shape[:-2] + (HALF, LANES))


def on_device(
    visibilities,
    hour_angle,
    antenna_layout_coords,
    point_coords,
    point_flux,
    counts,
    peel_order,
    earlier_gain_amplitude,
    earlier_gain_phase,
    tile_blocks,
):
    sections, dirs = point_coords.shape[0], lax.axis_size("dir")
    pols, tiles = lax.axis_size("pol"), lax.axis_size("bl")
    group = dirs * pols
    comps = point_flux.shape[1]
    intervals, total_times = visibilities.shape[0], visibilities.shape[3]
    times = total_times // dirs
    me_dir = lax.axis_index("dir")
    assert group % intervals == 0 and group >= intervals

    vis = visibilities.reshape(intervals, total_times, 2, HALF, LANES)
    vis = vis.transpose(0, 1, 3, 2, 4).reshape(intervals, total_times, ABLK, LANES)
    hours = lax.dynamic_slice_in_dim(hour_angle[:, 0], me_dir * times, times, 1)
    hour_cos, hour_sin = jnp.cos(hours)[..., None], jnp.sin(hours)[..., None]
    coords = point_coords[peel_order]
    live = counts[peel_order]
    weight = point_flux[peel_order] * (jnp.arange(comps)[None] < live[:, None]).astype(jnp.float32)
    l_row, m_row = coords[None, :, 0, None, :], coords[None, :, 1, None, :]
    hour_cos, hour_sin = hour_cos[:, None], hour_sin[:, None]
    east = l_row * hour_cos + m_row * hour_sin
    north = m_row * hour_cos - l_row * hour_sin
    chunks = jnp.clip((live + CHUNK - 1) // CHUNK, 1, comps // CHUNK)
    scalars = jnp.concatenate([me_dir[None], chunks]).astype(jnp.int32)

    left_block, right_block = tile_blocks[0, 0], tile_blocks[0, 1]

    def block_of(values, block):
        return lax.dynamic_slice_in_dim(values, block * ABLK, ABLK, values.ndim - 1)

    left_pos = block_of(antenna_layout_coords, left_block)
    left_pos = left_pos.reshape(2, HALF, 2).transpose(0, 2, 1).reshape(2, ABLK)
    positions = jnp.concatenate([left_pos, block_of(antenna_layout_coords, right_block)], axis=0)
    positions = jnp.broadcast_to(positions[:, :, None], (4, ABLK, CHUNK))
    prior_sides = []
    for block in (left_block, right_block):
        amplitude = block_of(earlier_gain_amplitude, block)[peel_order]
        angle = block_of(earlier_gain_phase, block)[peel_order]
        prior_sides += [amplitude * jnp.cos(angle), amplitude * jnp.sin(angle)]
    prior = outer_gains(*prior_sides)

    count = 3 * sections + sections * (sections - 1)
    rows = count * HALF
    whole = lambda shape: pl.BlockSpec(shape, lambda i, s: (0,) * len(shape))
    vis_spec = pl.BlockSpec((1, times, ABLK, LANES), lambda i, s: (i, s[0], 0, 0))
    model_spec = pl.BlockSpec(
        (1, sections, times, 2, HALF, LANES), lambda i, s: (i, 0, 0, 0, 0, 0)
    )
    row_spec = pl.BlockSpec((1, sections, times, comps), lambda i, s: (i, 0, 0, 0))
    limit = 48 * 1024 * 1024
    model, sums = pl.pallas_call(
        functools.partial(model_kernel, sections, times, comps, 2),
        out_shape=(
            jax.ShapeDtypeStruct((intervals, sections, times, 2, HALF, LANES), jnp.float32),
            jax.ShapeDtypeStruct((intervals, rows, LANES), jnp.float32),
        ),
        grid_spec=pltpu.PrefetchScalarGridSpec(
            num_scalar_prefetch=1,
            grid=(intervals,),
            in_specs=[
                whole((4, ABLK, CHUNK)),
                row_spec,
                row_spec,
                whole((sections, 1, comps)),
                whole((sections, 2, HALF, LANES)),
                vis_spec,
            ],
            out_specs=(
                model_spec,
                pl.BlockSpec((1, rows, LANES), lambda i, s: (i, 0, 0)),
            ),
        ),
        compiler_params=pltpu.CompilerParams(vmem_limit_bytes=limit),
        name="models",
    )(scalars, positions, east, north, weight[:, None], prior, vis)

    ids = jnp.concatenate([tile_blocks[0], jnp.zeros((6,), jnp.int32)]).astype(jnp.float32)
    ids = jnp.broadcast_to(ids[:, None], (8, LANES))
    vmem = pl.BlockSpec(memory_space=pltpu.VMEM)
    dma = pltpu.SemaphoreType.DMA
    gains = pl.pallas_call(
        functools.partial(solve_kernel, sections, intervals, tiles, dirs, pols),
        out_shape=jax.ShapeDtypeStruct((intervals, sections, 4, ABLK), jnp.float32),
        in_specs=[vmem, vmem],
        out_specs=vmem,
        scratch_shapes=[
            pltpu.VMEM((group - 1, rows, LANES), jnp.float32),
            pltpu.VMEM((tiles, rows + 8, LANES), jnp.float32),
            pltpu.VMEM((group, sections, 8, LANES), jnp.float32),
            pltpu.VMEM((tiles, 5, ABLK, LANES), jnp.float32),
            pltpu.VMEM((2, 2 * tiles, ABLK), jnp.float32),
            pltpu.VMEM((3, 2 * tiles, ABLK), jnp.float32),
            pltpu.VMEM((sections, 2, 2 * tiles, ABLK), jnp.float32),
            dma((group - 1,)),
            dma((group - 1,)),
            dma((tiles - 1,)),
            dma((tiles - 1,)),
            dma((group - 1,)),
            dma((group - 1,)),
        ],
        compiler_params=pltpu.CompilerParams(
            collective_id=0, has_side_effects=True, vmem_limit_bytes=56 * 1024 * 1024
        ),
        name="solve",
    )(sums, ids)

    factor = prior[None] - outer_gains(
        gains[:, :, 0], gains[:, :, 1], gains[:, :, 2], gains[:, :, 3]
    )
    out = pl.pallas_call(
        functools.partial(residual_kernel, sections, times),
        out_shape=jax.ShapeDtypeStruct((intervals, times, ABLK, LANES), jnp.float32),
        grid_spec=pltpu.PrefetchScalarGridSpec(
            num_scalar_prefetch=1,
            grid=(intervals,),
            in_specs=[
                vis_spec,
                model_spec,
                pl.BlockSpec((1, sections, 2, HALF, LANES), lambda i, s: (i, 0, 0, 0, 0)),
            ],
            out_specs=pl.BlockSpec((1, times, ABLK, LANES), lambda i, s: (i, 0, 0, 0)),
        ),
        compiler_params=pltpu.CompilerParams(vmem_limit_bytes=limit),
        name="residual",
    )(scalars, vis, model, factor)
    out = out.reshape(intervals, times, HALF, 2, LANES).transpose(0, 1, 3, 2, 4)
    return out.reshape(intervals, 1, 1, times, 2, HALF * LANES)


def solution(mesh):
    placed = (
        P("band", "bl", "pol", None, None, None),
        P(None, "pol", None),
        P(),
        P(),
        P(),
        P(),
        P(),
        P("band", None),
        P("band", None),
        P("bl", None),
    )
    return jax.shard_map(
        on_device,
        mesh=mesh,
        in_specs=placed,
        out_specs=P("band", "bl", "pol", "dir", None, None),
        check_vma=False,
    )
```

time: 863 us -> 95.9 us (0.11)
  waiting for transfers between devices: 510 us -> 0 us
  other arithmetic: 213 us -> 2.07 us
  matrix products: 79 us -> 0 us
  Pallas kernels: 0 us -> 76.7 us
  local copies, waits for them, and re-layouts: 41.3 us -> 16.4 us
  between operations: 13.5 us -> 1.34 us
    psum x6 -> x0, waiting for transfers between devices: 510 us -> none  [total_all(): return lax.psum(normals, ('bl', 'dir', 'pol'))]
    convert_element_type x2 -> x1, other arithmetic: 135 us -> 0.66 us  [on_device(): jnp.concatenate([tile_blocks[0], jnp.zeros((6,), jnp.int32)])]
    dot_general x106 -> x0, matrix products: 79 us -> none  [the longest x42 29.8 us: select_blocks(): jnp.einsum('kn,...np->...kp', onehot, grouped, precision=lax.Precision.HI...]
    pallas_call x0 -> x3, Pallas kernels: none -> 76.7 us  [the longest x1 38.7 us: on_device(): pl.pallas_call(functools.partial(model_kernel, sections, times, comps, 2)...]
    neg x2 -> x0, other arithmetic: 62.8 us -> none  [model_padded(): -left_real_component]
    reshape x11 -> x2, local copies, waits for them, and re-layouts: 14.8 us -> 0.18 us  [on_device(): left_pos = left_pos.reshape(2, HALF, 2).transpose(0, 2, 1).reshape(2, ABLK)]
    squeeze x4 -> x0, local copies, waits for them, and re-layouts: 10.5 us -> none  [the longest x2 6.16 us: peel_update(): current[:, :, :, 1] + (outer_real * model_imag + outer_imag * model_real)]
  transfers between devices with their start and end apart: 6 -> 0, of which waited for: 6 -> 0; matrix products, arithmetic and copies ran while one was open for 1% -> 0% of each run, Pallas kernels for 0% -> 0%
where the time goes in v1:
time: 95.9 us; the launch traced here: 96.5 us
  Pallas kernels  76.7 us (80%)
  local copies, waits for them, and re-layouts  16.4 us (17%)
  other arithmetic  2.07 us (2%)
  between operations  1.34 us (1%)
    pallas_call x1, Pallas kernels, on_device(): pl.pallas_call(functools.partial(model_kernel, sections, times, comps, 2)...  38.7 us
    pallas_call x1, Pallas kernels, on_device(): pl.pallas_call(functools.partial(solve_kernel, sections, intervals, tiles...  32.8 us
    pallas_call x1, Pallas kernels, on_device(): pl.pallas_call(functools.partial(residual_kernel, sections, times), out_s...  5.13 us
    unnamed x9, local copies, waits for them, and re-layouts  4.95 us

profile of v1, /device:TPU:0, one launch (start us, length us, event | category | flops | bytes accessed | tf_op | source)
XLA Modules:
  0.0 96.5 jit_solution(15242240854470188420)
XLA Ops:
  0.0 0.0 copy-start
  0.0 0.7 compare_select_fusion.1
  0.7 0.7 pad_convert_fusion
  1.3 1.3 %fusion.5 = (s32[1,1]{1,0:T(1,128)}, s32[1,1]{1,0:T(1,128)}) fusion(s32[1,2]{1,0:T(1,128)} %param.19), kind=kLoop, calls=%fused_computation.44 | loop fusion | bytes 16 | tf_op jit(solution)/shard_map/slice | solution.py:444
  3.8 0.8 constant_dynamic-slice_fusion.6
  4.6 0.8 constant_dynamic-slice_fusion.2
  5.4 0.6 gather_fusion.6
  5.9 0.6 gather_fusion.5
  6.5 0.6 gather_fusion.4
  7.1 0.6 gather_fusion.3
  7.7 1.3 %gather_fusion = s32[2]{0:T(128)S(1)} fusion(s32[2]{0:T(128)} %param.15, s32[1024]{0:T(1024)S(1)} %pad_clamp_fusion), kind=kCustom, calls=%fused_computation | custom fusion | bytes 24 | tf_op jit(solution)/shard_map/gather | solution.py:435
  9.0 0.1 pad_add_fusion.scalars
  9.1 0.7 broadcast_in_dim.11.ids_ref
  9.8 0.8 fusion.1
  10.6 1.3 %gather_fusion.2 = f32[2,512]{1,0:T(2,128)S(1)} fusion(f32[2,512]{1,0:T(2,128)} %param.14, s32[1024]{0:T(1024)S(1)} %pad_clamp_fusion), kind=kCustom, calls=%fused_computation.2 | custom fusion | bytes 8200 | tf_op jit(solution)/shard_map/gather | solution.py:436
  11.8 0.1 compare_select_fusion.weight_ref
  11.9 0.0 copy-done
  11.9 0.6 gather_fusion.1
  12.5 0.1 reshape.397
  12.6 0.1 copy.15
  12.7 0.1 reshape.398
  12.8 0.1 multiply_add_fusion.2
  12.9 0.1 add.77
  13.0 0.1 add.76
  13.1 0.1 sub.66
  13.1 0.1 sub.65
  13.2 0.1 broadcast_in_dim.10.pos_ref
  13.3 0.1 multiply_subtract_fusion.1
  13.5 38.7 %models.1 = (f32[4,2,16,2,32,128]{5,4,3,2,1,0:T(8,128)S(1)}, f32[4,256,128]{2,1,0:T(8,128)S(1)}) custom-call(s32[3]{0:T(128)S(1)} %pad_add_fusion.scalars, f32[4,64,128]{2,1,0:T(8,128)S(1)} %broadcast_in_dim.10.pos_ref, f32[4,2,16,512]{3,2,1,0:T(8,128)S(1)} %get-tuple-element.22.east_ref, f32[4,2,16,512]{3,2,1,0:T(8,128)S(1)} %get-tuple-element.21.north_ref, ...), custom_call_target="tpu_custom_call" | custom-call | tf_op jit(solution)/shard_map/models/pallas_call | solution.py:469
  52.2 0.0 copy-start.2
  52.2 2.0 %copy-done.2 = f32[4,2,16,2,32,128]{5,4,3,2,1,0:T(8,128)} copy-done((f32[4,2,16,2,32,128]{5,4,3,2,1,0:T(8,128)}, f32[4,2,16,2,32,128]{5,4,3,2,1,0:T(8,128)S(1)}, u32[]{:S(2)}) %copy-start.2) | copy-done | bytes 4194328
  54.2 0.0 copy-start.3
  54.2 0.8 copy-done.3
  55.0 32.8 %solve.1 = f32[4,2,4,64]{3,2,1,0:T(4,128)} custom-call(f32[4,256,128]{2,1,0:T(8,128)} %copy-done.3, f32[8,128]{1,0:T(8,128)} %broadcast_in_dim.11.ids_ref), custom_call_target="tpu_custom_call" | custom-call | tf_op jit(solution)/shard_map/solve/pallas_call | solution.py:499
  87.8 0.9 fusion.3
  88.7 0.2 multiply_add_fusion
  88.9 0.1 add.79
  89.0 0.1 sub.70
  89.2 0.0 copy-start.1
  89.2 2.2 %copy-done.1 = f32[4,1,1,32,2,4096]{5,4,3,2,1,0:T(2,128)S(1)} copy-done((f32[4,1,1,32,2,4096]{5,4,3,2,1,0:T(2,128)S(1)}, f32[4,1,1,32,2,4096]{5,4,3,2,1,0:T(2,128)}, u32[]{:S(2)}) %copy-start.1) | copy-done | bytes 4194328
  91.3 5.1 %residual.1 = f32[4,16,64,128]{3,2,1,0:T(8,128)} custom-call(s32[3]{0:T(128)S(1)} %pad_add_fusion.scalars, f32[4,32,64,128]{3,2,1,0:T(8,128)S(1)} %bitcast.32, f32[4,2,16,2,32,128]{5,4,3,2,1,0:T(8,128)} %copy-done.2, f32[4,2,2,32,128]{4,3,2,1,0:T(8,128)S(1)} %maximum_subtract_fusion.factor_ref), custom_call_target="tpu_custom_call" | custom-call | tf_op jit(solution)/shard_map/residual/pallas_call | solution.py:528
  (10 shorter events, 0.2 us)
Async XLA Ops:
  0.0 11.9 %copy-start = (f32[2,2,512]{2,1,0:T(2,128)S(1)}, f32[2,2,512]{2,1,0:T(2,128)}, u32[]{:S(2)}) copy-start(f32[2,2,512]{2,1,0:T(2,128)} %param.13) | copy-start | bytes 24580
  52.2 2.0 %copy-start.2 = (f32[4,2,16,2,32,128]{5,4,3,2,1,0:T(8,128)}, f32[4,2,16,2,32,128]{5,4,3,2,1,0:T(8,128)S(1)}, u32[]{:S(2)}) copy-start(f32[4,2,16,2,32,128]{5,4,3,2,1,0:T(8,128)S(1)} %get-tuple-element.7.model_ref) | copy-start | bytes 12582916
  54.2 0.8 copy-start.3
  89.2 2.2 %copy-start.1 = (f32[4,1,1,32,2,4096]{5,4,3,2,1,0:T(2,128)S(1)}, f32[4,1,1,32,2,4096]{5,4,3,2,1,0:T(2,128)}, u32[]{:S(2)}) copy-start(f32[4,1,1,32,2,4096]{5,4,3,2,1,0:T(2,128)} %param.10) | copy-start | bytes 12582916
